TPU v7x, 32 devices: a whole 2x2x4 slice. The times are simulated.
32 devices in a mesh: tm: 8 (over y, x, core), tile: 4 (over z).
Axes of the slice: x: 2, y: 2, z: 4, core: 2. Of those that a mesh axis runs over, the one named last changes fastest.
Arguments:
- velocity_u: float32 [384, 2, 16, 1024], P('tm', None, None, 'tile'), may hold values from -12 to 12
- velocity_v: float32 [384, 2, 16, 1024], P('tm', None, None, 'tile'), may hold values from -12 to 12
- land_sea: int32 [16, 1024], P(None, 'tile'), may hold values 0 or 1
- bottom_level: int32 [16, 1024], P(None, 'tile'), may hold values from 0 to 2
- spacing_x: float32 [16, 1024], P(None, 'tile'), may hold values from 0.5 to 2
- spacing_y: float32 [16, 1024], P(None, 'tile'), may hold values from 0.5 to 2
Outputs:
- conversion_maps: bfloat16 [384, 2, 16, 1024], P('tm', None, None, 'tile')
- mean_map: float32 [2, 16, 1024], P(None, None, 'tile')
All inputs are finite; a program needn't handle non-finite values. No bound on the sum of `land_sea` on one device may be relied on, other than what follows from the above.
Results may differ from a plain program's by a relative error of at most 0.001.
Values sent between devices are 32-bit elements; how exact they have to be, the bound alone decides.
A program may use at most 64 MiB of HBM per device.

v0:
```python
import jax
import jax.numpy as jnp
from jax import lax
from jax.sharding import PartitionSpec as P

HALF = 24
SNAPS = 48


cutoff_freq = 1.0 / 40.0


def extended(x, sides, width):
    for axis, dim in sides:
        size, length = (lax.axis_size(axis), x.shape[dim])
        up = [(i, (i + 1) % size) for i in range(size - 1)]
        down = [(j, i) for i, j in up]
        last = lax.slice_in_dim(x, length - width, length, axis=dim)
        first = lax.slice_in_dim(x, 0, width, axis=dim)
        before = lax.ppermute(last, axis, up)
        after = lax.ppermute(first, axis, down)
        x = jnp.concatenate([before, x, after], axis=dim)
    return x


def band_matrix(count):
    out_rows = jnp.arange(count, dtype=jnp.int32)[:, None]
    in_cols = jnp.arange(count + 2 * HALF, dtype=jnp.int32)[None, :]
    offset = (in_cols - out_rows - HALF).astype(jnp.float32)
    weights = 2.0 * cutoff_freq * jnp.sinc(2.0 * cutoff_freq * offset) * jnp.sinc(offset / HALF)
    return jnp.where(jnp.abs(offset) <= HALF, weights, jnp.zeros_like(weights))


def lowpass(padded, validity, blocks, block):
    matrix = band_matrix(block)

    def one_block(block_id):
        start = block_id * block
        window = lax.dynamic_slice_in_dim(padded, start, block + 2 * HALF, 0)
        valid_part = lax.dynamic_slice_in_dim(validity, start, block + 2 * HALF, 0)
        weighted = jnp.dot(
            matrix, window, precision=lax.Precision.HIGHEST, preferred_element_type=jnp.float32
        )
        weight_sum = jnp.dot(
            matrix, valid_part, precision=lax.Precision.HIGHEST, preferred_element_type=jnp.float32
        )
        return weighted / weight_sum[:, None]

    result = lax.map(one_block, jnp.arange(blocks, dtype=jnp.int32))
    return result.reshape(blocks * block, padded.shape[1])


def wet_cells(land_sea, bottom_level, levels):
    level_ids = jnp.arange(levels, dtype=jnp.int32)[:, None, None]
    return ((land_sea[None] == 1) & (level_ids < bottom_level[None])).astype(jnp.float32)


def filter_series(series):
    length = series.shape[0]
    flattened = series.reshape(length, -1)
    padded = jnp.pad(flattened, ((HALF, HALF), (0, 0)))
    validity = jnp.pad(jnp.ones((length,), jnp.float32), (HALF, HALF))
    return lowpass(padded, validity, length // SNAPS, SNAPS).reshape(series.shape)


def shards(velocity_u, velocity_v, land_sea, bottom_level, spacing_x, spacing_y):
    block_len = velocity_u.shape[0]
    total_len = block_len * lax.axis_size("tm")
    stacked = jnp.stack([velocity_u, velocity_v], axis=1)
    full_shape = stacked.shape
    flat_cells = stacked.reshape(block_len, 2, -1)
    series_mean = filter_series(
        lax.all_to_all(flat_cells, "tm", split_axis=2, concat_axis=0, tiled=True)
    )
    mean_flat = lax.all_to_all(series_mean, "tm", split_axis=0, concat_axis=2, tiled=True)
    mean_flow = mean_flat.reshape(full_shape)
    eddies = stacked - mean_flow
    wet_mask = wet_cells(land_sea, bottom_level, full_shape[2])
    masked = mean_flow * wet_mask[None, None]
    edge_cols = jnp.concatenate([masked[..., :1], masked[..., -1:]], axis=4)
    edge_ext = extended(edge_cols, (("tile", 4),), 1)
    left_col = edge_ext[..., :1]
    right_col = edge_ext[..., 3:4]
    ahead = jnp.concatenate([masked[..., 1:], right_col], axis=4)
    behind = jnp.concatenate([left_col, masked[..., :-1]], axis=4)
    grad_x = (ahead - behind) * (0.5 / spacing_x)
    row_padded = jnp.pad(masked, ((0, 0), (0, 0), (0, 0), (1, 1), (0, 0)))
    grad_y = (row_padded[..., 2:, :] - row_padded[..., :-2, :]) * (0.5 / spacing_y)
    eddy_u = eddies[:, 0]
    eddy_v = eddies[:, 1]
    total = (
        eddy_u * eddy_u * grad_x[:, 0]
        + eddy_u * eddy_v * (grad_y[:, 0] + grad_x[:, 1])
        + eddy_v * eddy_v * grad_y[:, 1]
    )
    conversion = -wet_mask[None] * total
    summed = lax.psum(jnp.sum(conversion, axis=0), "tm")
    return (conversion.astype(jnp.bfloat16), summed / total_len)


def solution(mesh):
    in_specs = (
        P("tm", None, None, "tile"),
        P("tm", None, None, "tile"),
        P(None, "tile"),
        P(None, "tile"),
        P(None, "tile"),
        P(None, "tile"),
    )
    out_specs = (P("tm", None, None, "tile"), P(None, None, "tile"))
    return jax.shard_map(shards, mesh=mesh, in_specs=in_specs, out_specs=out_specs, check_vma=False)
```

profile of v0, /device:TPU:0, one launch (start us, length us, event | category | flops | bytes accessed | tf_op | source)
XLA Modules:
  0.0 262.5 jit_solution(6098952019784487532)
XLA Ops:
  0.6 0.0 copy-start.3
  0.6 2.7 %stack.18 = f32[48,1,8192]{2,0,1:T(8,128)} reshape(f32[48,2,16,256]{3,2,1,0:T(8,128)} %param.9) | data formatting | bytes 3145728 | tf_op jit(solution)/shard_map/stack | solution.py:69
  3.3 1.4 stack.19
  4.8 2.1 pad_maximum_fusion
  6.9 8.0 %copy.21 = f32[48,2,8192]{0,1,2:T(2,128)} copy(f32[48,2,8192]{2,0,1:T(8,128)S(1)} %pad_maximum_fusion) | data formatting | bytes 6291456 | tf_op jit(solution)/shard_map/stack | solution.py:69
  14.9 16.2 %reshape.50 = f32[8,1,98304]{2,1,0:T(1,128)} reshape(f32[8192,2,48]{2,1,0:T(2,128)} %bitcast.49) | data formatting | bytes 6291456
  31.0 5.7 %all-to-all-start = ((f32[8,1,98304]{2,1,0:T(1,128)}), f32[8,1,98304]{2,1,0:T(1,128)S(1)}, u32[]{:S(2)}, u32[]{:S(2)}) async-start(f32[8,1,98304]{2,1,0:T(1,128)} %reshape.50), calls=%async_computation | async-start | bytes 6291456 | tf_op jit(solution)/shard_map/all_to_all | solution.py:73
  36.7 0.1 pad.13
  36.8 0.7 fusion.42
  37.5 36.6 %all-to-all-done = f32[8,1,98304]{2,1,0:T(1,128)S(1)} async-done(((f32[8,1,98304]{2,1,0:T(1,128)}), f32[8,1,98304]{2,1,0:T(1,128)S(1)}, u32[]{:S(2)}, u32[]{:S(2)}) %all-to-all-start) | async-done | bytes 3145760 | tf_op jit(solution)/shard_map/all_to_all | solution.py:73
  74.1 0.5 broadcast.65
  74.6 11.2 %reduce = f32[8,98304]{1,0:T(8,128)} reduce(f32[8,1,98304]{2,1,0:T(1,128)S(1)} %all-to-all-done, f32[]{:T(128)} %broadcast.65), dimensions={1}, to_apply=%all_to_all.22.reduce_sub_computation | reduce | bytes 6291460 | tf_op jit(solution)/shard_map/all_to_all | solution.py:73
  85.8 19.0 %reshape.51 = f32[8192,2,48]{2,1,0:T(2,128)} reshape(f32[8,98304]{1,0:T(8,128)} %reduce) | data formatting | bytes 6291456
  104.8 7.0 %copy.30 = f32[48,2,8,1024]{3,2,0,1:T(8,128)S(1)} copy(f32[48,2,8,1024]{0,1,3,2:T(2,128)} %bitcast.50) | data formatting | bytes 6291456 | tf_op jit(solution)/shard_map/all_to_all | solution.py:73
  111.7 2.4 copy.23
  114.2 1.4 copy.31
  115.6 0.4 pad.12
  116.0 34.3 %while.11 = (s32[]{:T(128)}, f32[8,48,2048]{2,1,0:T(8,128)}, s32[8]{0:T(128)S(1)}, f32[432,2048]{1,0:T(8,128)S(1)}, f32[48,96]{1,0:T(8,128)}, /*index=5*/f32[432...) while((s32[]{:T(128)}, f32[8,48,2048]{2,1,0:T(8,128)}, s32[8]{0:T(128)S(1)}, ...), condition=%wide.region_1.3_spmd.clone, body=%wide.region_0.2_spmd.clone.sunk | while | flops 113399816 | bytes 1224551 | solution.py:49
  116.0 0.6 dynamic_slice.24
  117.3 0.9 convolution_bitcast_fusion.2
  118.2 2.1 fusion.59
  120.3 0.6 dynamic_slice.24
  121.6 0.9 convolution_bitcast_fusion.2
  122.5 2.1 fusion.59
  124.6 0.6 dynamic_slice.24
  125.9 0.9 convolution_bitcast_fusion.2
  126.8 2.1 fusion.59
  128.9 0.6 dynamic_slice.24
  130.1 0.9 convolution_bitcast_fusion.2
  131.1 2.1 fusion.59
  133.2 0.6 dynamic_slice.24
  134.4 0.9 convolution_bitcast_fusion.2
  135.4 2.1 fusion.59
  137.4 0.6 dynamic_slice.24
  138.7 0.9 convolution_bitcast_fusion.2
  139.6 2.1 fusion.59
  141.7 0.6 dynamic_slice.24
  143.0 0.9 convolution_bitcast_fusion.2
  143.9 2.1 fusion.59
  146.0 0.6 dynamic_slice.24
  147.3 0.9 convolution_bitcast_fusion.2
  148.2 2.1 fusion.59
  150.3 5.6 %reshape_reshape.3 = f32[384,2,1024]{2,1,0:T(2,128)} reshape(f32[8,48,2048]{2,1,0:T(8,128)} %get-tuple-element.38) | data formatting | bytes 6291456 | tf_op jit(solution)/shard_map/reshape;reshape | solution.py:63
  155.9 4.0 %all-to-all-start.1 = ((f32[384,2,1024]{2,1,0:T(2,128)}), f32[384,2,1024]{2,1,0:T(2,128)S(1)}, u32[]{:S(2)}, u32[]{:S(2)}) async-start(f32[384,2,1024]{2,1,0:T(2,128)} %reshape_reshape.3), calls=%async_computation.1 | async-start | bytes 6291456 | tf_op jit(solution)/shard_map/all_to_all | solution.py:75
  160.0 37.7 %all-to-all-done.1 = f32[384,2,1024]{2,1,0:T(2,128)S(1)} async-done(((f32[384,2,1024]{2,1,0:T(2,128)}), f32[384,2,1024]{2,1,0:T(2,128)S(1)}, u32[]{:S(2)}, u32[]{:S(2)}) %all-to-all-start.1) | async-done | bytes 3145760 | tf_op jit(solution)/shard_map/all_to_all | solution.py:75
  197.7 1.0 copy.24
  198.7 1.8 copy.25
  200.5 2.6 reshape.47
  203.1 5.7 %maximum_subtract_fusion = (f32[48,2,2,16,256]{4,3,2,1,0:T(8,128)}, f32[48,2,2,16,256]{4,3,2,1,0:T(8,128)S(1)}) fusion(f32[48,2,2,16,256]{4,3,2,1,0:T(8,128)} %reshape.47, f32[48,1,2,16,256]{4,3,2,1,0:T(8,128)} %bitcast.55, f32[48,1,2,16,256]{4,3,2,1,0:T(8,128)} %bitcast.56, f32[2,16,256]{2,1,0:T(8,128)S(1)} %fusion.15), kind=kLoop, calls=%fused_computation.12 | loop fusion | flops 2359296 | bytes 12615680 | tf_op jit(solution)/shard_map/sub | solution.py:77
  208.8 3.7 %fusion.47 = (f32[48,2,2,16,255]{4,3,2,1,0:T(8,128)}, f32[48,2,2,16,255]{4,3,2,1,0:T(8,128)}) fusion(f32[48,2,2,16,256]{4,3,2,1,0:T(8,128)S(1)} %get-tuple-element.70), kind=kLoop, calls=%fused_computation.85 | loop fusion | bytes 12533760 | tf_op jit(solution)/shard_map/slice | solution.py:85
  212.5 2.3 fusion.46
  214.8 2.2 copy.26
  217.0 1.3 collective-permute-start
  218.3 2.2 copy.28
  220.4 4.8 %collective-permute-start.1 = (f32[48,2,2,16,1]{0,3,4,2,1:T(8,128)S(1)}, f32[48,2,2,16,1]{0,3,4,2,1:T(8,128)S(1)}, u32[]{:S(2)}, u32[]{:S(2)}) collective-permute-start(f32[48,2,2,16,1]{0,3,4,2,1:T(8,128)S(1)} %copy.28), channel_id=1, source_target_pairs={{0,1},{1,2},{2,3},{4,5},{5,6},{6,7},{8,9},{9,10},{10,11},{12,13},{... | collective-permute-start | bytes 36872 | tf_op jit(solution)/shard_map/ppermute | solution.py:20
  225.2 2.4 fusion.7
  227.7 0.0 collective-permute-done
  227.7 2.4 copy.27
  230.1 2.4 copy.29
  232.4 4.3 %fusion.8 = f32[48,2,2,16,256]{4,3,2,1,0:T(8,128)S(1)} fusion(f32[48,2,2,16,1]{4,3,2,1,0:T(8,128)} %copy.27, f32[48,2,2,16,255]{4,3,2,1,0:T(8,128)} %get-tuple-element.74, f32[48,2,2,16,255]{4,3,2,1,0:T(8,128)S(1)} %copy-done.2, f32[48,2,2,16,1]{4,3,2,1,0:T(8,128)} %copy.29, f32[16,256]{1,0:T(8,128)S(1)} %broadcast_divide_fusion.1), kind=kLoop, calls=%fused_computation.15 | loop fusion | flops 3145728 | bytes 9453568 | tf_op jit(solution)/shard_map/mul | solution.py:86
  236.8 0.4 copy-done.1
  237.1 2.1 fusion.44
  239.3 22.3 %psum.7 = f32[2,16,256]{2,1,0:T(8,128)S(1)} all-reduce(f32[2,16,256]{2,1,0:T(8,128)S(1)} %get-tuple-element.67), channel_id=1, replica_groups=mesh['tm'=8,'tile'=4] {'tm'}, use_global_device_ids=true, to_apply=%region_3.5 | all-reduce | flops 8192 | bytes 65536 | tf_op jit(solution)/shard_map/psum | solution.py:97
  261.6 0.6 broadcast_multiply_fusion.1
  (23 shorter events, 0.1 us)
Async XLA Ops:
  0.6 2.7 %copy-start.3 = (f32[48,2,16,256]{3,2,1,0:T(8,128)S(1)}, f32[48,2,16,256]{3,2,1,0:T(8,128)}, u32[]{:S(2)}) copy-start(f32[48,2,16,256]{3,2,1,0:T(8,128)} %param.10) | copy-start | bytes 4718596
  31.0 43.1 %all-to-all-start = ((f32[8,1,98304]{2,1,0:T(1,128)}), f32[8,1,98304]{2,1,0:T(1,128)S(1)}, u32[]{:S(2)}, u32[]{:S(2)}) async-start(f32[8,1,98304]{2,1,0:T(1,128)} %reshape.50), calls=%async_computation | async-start | bytes 6291456 | tf_op jit(solution)/shard_map/all_to_all | solution.py:73
  155.9 4.0 %copy-start.5 = (s32[16,256]{1,0:T(8,128)S(1)}, s32[16,256]{1,0:T(8,128)}, u32[]{:S(2)}) copy-start(s32[16,256]{1,0:T(8,128)} %param.11) | copy-start | bytes 49156
  155.9 4.1 %copy-start.6 = (f32[16,256]{1,0:T(8,128)S(1)}, f32[16,256]{1,0:T(8,128)}, u32[]{:S(2)}) copy-start(f32[16,256]{1,0:T(8,128)} %param.13) | copy-start | bytes 49156
  155.9 4.1 %copy-start.7 = (f32[16,256]{1,0:T(8,128)S(1)}, f32[16,256]{1,0:T(8,128)}, u32[]{:S(2)}) copy-start(f32[16,256]{1,0:T(8,128)} %param.14) | copy-start | bytes 49156
  155.9 4.1 %copy-start.4 = (s32[16,256]{1,0:T(8,128)S(1)}, s32[16,256]{1,0:T(8,128)}, u32[]{:S(2)}) copy-start(s32[16,256]{1,0:T(8,128)} %param.12) | copy-start | bytes 49156
  155.9 41.8 %all-to-all-start.1 = ((f32[384,2,1024]{2,1,0:T(2,128)}), f32[384,2,1024]{2,1,0:T(2,128)S(1)}, u32[]{:S(2)}, u32[]{:S(2)}) async-start(f32[384,2,1024]{2,1,0:T(2,128)} %reshape_reshape.3), calls=%async_computation.1 | async-start | bytes 6291456 | tf_op jit(solution)/shard_map/all_to_all | solution.py:75
  217.0 10.7 %collective-permute-start = (f32[48,2,2,16,1]{0,3,4,2,1:T(8,128)S(1)}, f32[48,2,2,16,1]{0,3,4,2,1:T(8,128)S(1)}, u32[]{:S(2)}, u32[]{:S(2)}) collective-permute-start(f32[48,2,2,16,1]{0,3,4,2,1:T(8,128)S(1)} %copy.26), channel_id=1, source_target_pairs={{1,0},{2,1},{3,2},{5,4},{6,5},{7,6},{9,8},{10,9},{11,10},{13,12},{... | collective-permute-start | bytes 36872 | tf_op jit(solution)/shard_map/ppermute | solution.py:21
  220.4 9.6 %collective-permute-start.1 = (f32[48,2,2,16,1]{0,3,4,2,1:T(8,128)S(1)}, f32[48,2,2,16,1]{0,3,4,2,1:T(8,128)S(1)}, u32[]{:S(2)}, u32[]{:S(2)}) collective-permute-start(f32[48,2,2,16,1]{0,3,4,2,1:T(8,128)S(1)} %copy.28), channel_id=1, source_target_pairs={{0,1},{1,2},{2,3},{4,5},{5,6},{6,7},{8,9},{9,10},{10,11},{12,13},{... | collective-permute-start | bytes 36872 | tf_op jit(solution)/shard_map/ppermute | solution.py:20
  227.7 4.7 %copy-start.2 = (f32[48,2,2,16,255]{4,3,2,1,0:T(8,128)S(1)}, f32[48,2,2,16,255]{4,3,2,1,0:T(8,128)}, u32[]{:S(2)}) copy-start(f32[48,2,2,16,255]{4,3,2,1,0:T(8,128)} %get-tuple-element.73) | copy-start | bytes 9400324
  232.4 4.3 %copy-start = (f32[48,2,2,16,256]{4,3,2,1,0:T(8,128)S(1)}, f32[48,2,2,16,256]{4,3,2,1,0:T(8,128)}, u32[]{:S(2)}) copy-start(f32[48,2,2,16,256]{4,3,2,1,0:T(8,128)} %fusion.7) | copy-start | bytes 9437188
  232.4 4.7 %copy-start.1 = (f32[48,2,2,16,256]{4,3,2,1,0:T(8,128)S(1)}, f32[48,2,2,16,256]{4,3,2,1,0:T(8,128)}, u32[]{:S(2)}) copy-start(f32[48,2,2,16,256]{4,3,2,1,0:T(8,128)} %get-tuple-element.69) | copy-start | bytes 9437188
where the time goes:
time: 267 us; the launch traced here: 262 us
  local copies, waits for them, and re-layouts  90.4 us (34%)
  waiting for transfers between devices  74.3 us (28%)
  other arithmetic  29.2 us (11%)
  matrix products  24.2 us (9%)
  blocking collectives  22.3 us (8%)
  starting transfers between devices  15.7 us (6%)
  loops' own time  5.18 us (2%)
    all_to_all x1, waiting for transfers between devices, shards(): lax.all_to_all(series_mean, 'tm', split_axis=0, concat_axis=2, tiled=True)  37.7 us
    unnamed x19, local copies, waits for them, and re-layouts  37 us
    all_to_all x1, waiting for transfers between devices, shards(): lax.all_to_all(flat_cells, 'tm', split_axis=2, concat_axis=0, tiled=True)  36.6 us
    psum x1, blocking collectives, shards(): summed = lax.psum(jnp.sum(conversion, axis=0), 'tm')  22.3 us
    dot_general x8, matrix products, one_block(): jnp.dot(matrix, window, precision=lax.Precision.HIGHEST, preferred_elemen...  16.8 us
    another operation x3, local copies, waits for them, and re-layouts, shards(): stacked = jnp.stack([velocity_u, velocity_v], axis=1)  12.1 us
    all_to_all x1, other arithmetic, shards(): lax.all_to_all(flat_cells, 'tm', split_axis=2, concat_axis=0, tiled=True)  11.2 us
    all_to_all x3, local copies, waits for them, and re-layouts, shards(): lax.all_to_all(flat_cells, 'tm', split_axis=2, concat_axis=0, tiled=True)  9.91 us
  transfers between devices with their start and end apart: 4, of which 2 were waited for; matrix products, arithmetic and copies ran while one was open for 3% of the time, Pallas kernels for 0%

commit v1 on v0

v1 whole, which is shorter than its diff:
```python
import functools

import jax
import jax.numpy as jnp
import numpy as np
from jax import lax
from jax.experimental import pallas as pl
from jax.experimental.pallas import tpu as pltpu
from jax.sharding import PartitionSpec as P

HALF = 24
CUTOFF = 1.0 / 40.0
LANES = 128
CHUNK = 8
MESH = pl.DeviceIdType.MESH


def band_parts(count):
    offset = (np.arange(count + 2 * HALF)[None, :] - np.arange(count)[:, None] - HALF).astype(np.float64)
    weights = 2.0 * CUTOFF * np.sinc(2.0 * CUTOFF * offset) * np.sinc(offset / HALF)
    weights = np.where(np.abs(offset) <= HALF, weights, 0.0).astype(np.float32)
    own = weights[:, HALF : HALF + count]
    halo = np.concatenate([weights[:, :HALF], weights[:, HALF + count :]], axis=1)
    return own, halo


def dot(a, b):
    return jnp.dot(a, b, precision=lax.Precision.HIGHEST, preferred_element_type=jnp.float32)


def kernel(
    n_tm, n_tile, levels,
    u_ref, v_ref, land_ref, bottom_ref, sx_ref, sy_ref, own_ref, halo_w_ref,
    conv_ref, mean_ref,
    x, halo, mm, cf, wet, cx, cy, sums, part, edge, edge_halo, edge_mean, edge_in,
    x_sem, bulk_send, bulk_recv, edge_send, edge_recv, em_send, em_recv, part_send, part_recv,
):
    snaps, cells, width = u_ref.shape
    rows = cells // levels
    t = lax.axis_index("tm")
    z = lax.axis_index("tile")
    chunks = cells // CHUNK
    fields = (u_ref, v_ref)

    barrier = pltpu.get_barrier_semaphore()
    for k in range(1, n_tm):
        pl.semaphore_signal(barrier, inc=1, device_id={"tm": lax.rem(t + k, n_tm)}, device_id_type=MESH)

    @pl.when(z > 0)
    def _():
        pl.semaphore_signal(barrier, inc=1, device_id={"tile": z - 1}, device_id_type=MESH)

    @pl.when(z < n_tile - 1)
    def _():
        pl.semaphore_signal(barrier, inc=1, device_id={"tile": z + 1}, device_id_type=MESH)

    def local(f, h):
        return pltpu.make_async_copy(
            fields[f].at[:, :, pl.ds(h * LANES, LANES)], x.at[f, h], x_sem.at[f, h]
        )

    for f in range(2):
        for h in range(2):
            local(f, h).start()

    pl.semaphore_wait(barrier, n_tm - 1 + (z > 0).astype(jnp.int32) + (z < n_tile - 1).astype(jnp.int32))

    def bulk(side, c, f, h):
        first = snaps - HALF if side == 0 else 0
        to = t + 1 if side == 0 else t - 1
        return pltpu.make_async_remote_copy(
            src_ref=fields[f].at[pl.ds(first, HALF), pl.ds(c * CHUNK, CHUNK), pl.ds(h * LANES, LANES)],
            dst_ref=halo.at[side, f, h, :, pl.ds(c * CHUNK, CHUNK), :],
            send_sem=bulk_send.at[side, c, f, h],
            recv_sem=bulk_recv.at[side, c, f, h],
            device_id={"tm": to},
            device_id_type=MESH,
        )

    def edge_copy(side):
        first = snaps - HALF if side == 0 else 0
        to = t + 1 if side == 0 else t - 1
        return pltpu.make_async_remote_copy(
            src_ref=edge.at[pl.ds(first, HALF), :],
            dst_ref=edge_halo.at[side],
            send_sem=edge_send.at[side],
            recv_sem=edge_recv.at[side],
            device_id={"tm": to},
            device_id_type=MESH,
        )

    def mean_copy(side):
        to = z + 1 if side == 0 else z - 1
        return pltpu.make_async_remote_copy(
            src_ref=edge_mean,
            dst_ref=edge_in.at[side],
            send_sem=em_send.at[side],
            recv_sem=em_recv.at[side],
            device_id={"tile": to},
            device_id_type=MESH,
        )

    def part_copy(l, k, slot):
        return pltpu.make_async_remote_copy(
            src_ref=part.at[slot, l],
            dst_ref=part.at[slot, l],
            send_sem=part_send.at[l, k],
            recv_sem=part_recv.at[l, k],
            device_id={"tm": lax.rem(t + k, n_tm)},
            device_id_type=MESH,
        )

    sends = (t < n_tm - 1, t > 0)
    receives = (t > 0, t < n_tm - 1)
    z_sends = (z < n_tile - 1, z > 0)
    z_receives = (z > 0, z < n_tile - 1)

    for c in range(chunks):
        for side in range(2):

            @pl.when(sends[side])
            def _():
                for f in range(2):
                    for h in range(2):
                        bulk(side, c, f, h).start()

    for side in range(2):

        @pl.when(jnp.logical_not(receives[side]))
        def _():
            halo[side] = jnp.zeros(halo.shape[1:], jnp.float32)
            edge_halo[side] = jnp.zeros(edge_halo.shape[1:], jnp.float32)

        @pl.when(jnp.logical_not(z_receives[side]))
        def _():
            edge_in[side] = jnp.zeros(edge_in.shape[1:], jnp.float32)

    for l in range(levels):
        is_wet = (land_ref[...] == 1) & (l < bottom_ref[...])
        level_wet = jnp.where(is_wet, 1.0, 0.0).astype(jnp.float32)
        for j in range(rows):
            wet[l * rows + j] = level_wet[j : j + 1, :]
    all_x, all_y = 0.5 / sx_ref[...], 0.5 / sy_ref[...]
    for j in range(rows):
        cx[j] = all_x[j : j + 1, :]
        cy[j] = all_y[j : j + 1, :]
    for f in range(2):
        for l in range(levels):
            for j in (0, rows + 1):
                mm[f, l, j] = jnp.zeros((snaps, width), jnp.float32)
    column = lax.broadcasted_iota(jnp.int32, (snaps, 2 * HALF), 1)
    valid = ((column >= HALF) | (t > 0)) & ((column < HALF) | (t < n_tm - 1))
    own_w = own_ref[...]
    halo_w = jnp.where(valid, halo_w_ref[...], 0.0)
    weight_sum = jnp.sum(own_w, axis=1, keepdims=True) + jnp.sum(halo_w, axis=1, keepdims=True)
    own_w = own_w / weight_sum
    halo_w = halo_w / weight_sum

    for f in range(2):
        for h in range(2):
            local(f, h).wait()

    def series(ref, count, r):
        return ref.reshape(count * cells, LANES)[pl.ds(r, count, stride=cells), :]

    lane = lax.broadcasted_iota(jnp.int32, (snaps, LANES), 1)

    def pack(r, acc):
        for f in range(2):
            q = f * cells + r
            first = series(x.at[f, 0], snaps, r) * wet[r][:, :LANES]
            acc = jnp.where(lane == q, pltpu.roll(first, q, 1), acc)
            q = (2 + f) * cells + r
            last = series(x.at[f, 1], snaps, r) * wet[r][:, width - LANES :]
            acc = jnp.where(lane == q, pltpu.roll(last, lax.rem(q + 1, LANES), 1), acc)
        return acc

    edge[...] = lax.fori_loop(0, cells, pack, jnp.zeros((snaps, LANES), jnp.float32))
    for side in range(2):

        @pl.when(sends[side])
        def _():
            edge_copy(side).start()

    def own_part(r, carry):
        l, j = r // rows, lax.rem(r, rows)
        for f in range(2):
            block = jnp.concatenate([series(x.at[f, h], snaps, r) for h in range(2)], axis=1)
            mm[f, l, j + 1] = dot(own_w, block)
        return carry

    lax.fori_loop(0, cells, own_part, 0)

    for side in range(2):

        @pl.when(receives[side])
        def _():
            edge_copy(side).wait_recv()

    edge_mean[...] = dot(own_w, edge[...]) + dot(
        halo_w, jnp.concatenate([edge_halo[0], edge_halo[1]], axis=0)
    )
    for side in range(2):

        @pl.when(z_sends[side])
        def _():
            mean_copy(side).start()

    wide = lax.broadcasted_iota(jnp.int32, (snaps, width), 1)

    def halo_part(r, carry):
        l, j = r // rows, lax.rem(r, rows)
        mask = wet[r]
        for f in range(2):
            block = jnp.concatenate(
                [
                    jnp.concatenate([series(halo.at[s, f, h], HALF, r) for h in range(2)], axis=1)
                    for s in range(2)
                ],
                axis=0,
            )
            mm[f, l, j + 1] = (mm[f, l, j + 1] + dot(halo_w, block)) * mask
        return carry

    def grad_x(f, r, masked, scale):
        q = (2 + f) * cells + r
        before = pltpu.roll(edge_in[0], lax.rem(2 * LANES - q, LANES), 1)
        q = f * cells + r
        after = pltpu.roll(edge_in[1], lax.rem(2 * LANES - 1 - q, LANES), 1)
        before = jnp.concatenate([before, before], axis=1)
        after = jnp.concatenate([after, after], axis=1)
        behind = jnp.where(wide == 0, before, pltpu.roll(masked, 1, 1))
        ahead = jnp.where(wide == width - 1, after, pltpu.roll(masked, width - 1, 1))
        return (ahead - behind) * scale

    def convert(l):
        def body(j, carry):
            r = l * rows + j
            mask = wet[r]
            scale_x = cx[j]
            scale_y = cy[j]
            eddy, gx, gy = [], [], []
            for f in range(2):
                masked = mm[f, l, j + 1]
                raw = jnp.concatenate([series(x.at[f, h], snaps, r) for h in range(2)], axis=1)
                eddy.append(raw - masked)
                gx.append(grad_x(f, r, masked, scale_x))
                gy.append((mm[f, l, j + 2] - mm[f, l, j]) * scale_y)
            eu, ev = eddy
            total = eu * eu * gx[0] + eu * ev * (gy[0] + gx[1]) + ev * ev * gy[1]
            conversion = -mask * total
            for h in range(2):
                cf.at[h].reshape(snaps * cells, LANES)[pl.ds(r, snaps, stride=cells), :] = conversion[
                    :, h * LANES : (h + 1) * LANES
                ]
            sums[r] = jnp.sum(conversion, axis=0, keepdims=True)
            return carry

        return body

    per_level = rows // CHUNK
    for c in range(chunks):
        for side in range(2):

            @pl.when(receives[side])
            def _():
                for f in range(2):
                    for h in range(2):
                        bulk(side, c, f, h).wait_recv()

        lax.fori_loop(c * CHUNK, (c + 1) * CHUNK, halo_part, 0)
        if c == 0:
            for side in range(2):

                @pl.when(z_receives[side])
                def _():
                    mean_copy(side).wait_recv()

        l, piece = c // per_level, c % per_level
        low = piece * CHUNK - (1 if piece else 0)
        high = rows if piece == per_level - 1 else (piece + 1) * CHUNK - 1
        lax.fori_loop(low, high, convert(l), 0)
        if piece == per_level - 1:
            part[t, l] = jnp.concatenate([sums[l * rows + j] for j in range(rows)], axis=0)
            for k in range(1, n_tm):
                part_copy(l, k, t).start()

            def narrow(s, carry):
                for h in range(2):
                    conv_ref[s, pl.ds(l * rows, rows), pl.ds(h * LANES, LANES)] = cf[
                        h, s, pl.ds(l * rows, rows), :
                    ].astype(jnp.bfloat16)
                return carry

            lax.fori_loop(0, snaps, narrow, 0)

    for l in range(levels):
        for k in range(1, n_tm):
            part_copy(l, k, lax.rem(t + n_tm - k, n_tm)).wait_recv()
        total = part[0, l]
        for s in range(1, n_tm):
            total = total + part[s, l]
        mean_ref[l] = total / (snaps * n_tm)

    for side in range(2):

        @pl.when(sends[side])
        def _():
            edge_copy(side).wait_send()
            for c in range(chunks):
                for f in range(2):
                    for h in range(2):
                        bulk(side, c, f, h).wait_send()

        @pl.when(z_sends[side])
        def _():
            mean_copy(side).wait_send()

    for l in range(levels):
        for k in range(1, n_tm):
            part_copy(l, k, t).wait_send()


def shards(velocity_u, velocity_v, land_sea, bottom_level, spacing_x, spacing_y):
    snaps, levels, rows, width = velocity_u.shape
    cells = levels * rows
    n_tm, n_tile = lax.axis_size("tm"), lax.axis_size("tile")
    assert width == 2 * LANES and 4 * cells == LANES and snaps >= HALF and rows % CHUNK == 0
    own, halo = band_parts(snaps)
    chunks = cells // CHUNK
    vmem = pl.BlockSpec(memory_space=pltpu.VMEM)
    anywhere = pl.BlockSpec(memory_space=pl.ANY)
    f32 = jnp.float32
    dma = pltpu.SemaphoreType.DMA
    conversion, mean_map = pl.pallas_call(
        functools.partial(kernel, n_tm, n_tile, levels),
        out_shape=(
            jax.ShapeDtypeStruct((snaps, cells, width), jnp.bfloat16),
            jax.ShapeDtypeStruct((levels, rows, width), f32),
        ),
        in_specs=[anywhere] * 2 + [vmem] * 6,
        out_specs=(vmem, vmem),
        scratch_shapes=[
            pltpu.VMEM((2, 2, snaps, cells, LANES), f32),
            pltpu.VMEM((2, 2, 2, HALF, cells, LANES), f32),
            pltpu.VMEM((2, levels, rows + 2, snaps, width), f32),
            pltpu.VMEM((2, snaps, cells, LANES), f32),
            pltpu.VMEM((cells, 1, width), f32),
            pltpu.VMEM((rows, 1, width), f32),
            pltpu.VMEM((rows, 1, width), f32),
            pltpu.VMEM((cells, 1, width), f32),
            pltpu.VMEM((n_tm, levels, rows, width), f32),
            pltpu.VMEM((snaps, LANES), f32),
            pltpu.VMEM((2, HALF, LANES), f32),
            pltpu.VMEM((snaps, LANES), f32),
            pltpu.VMEM((2, snaps, LANES), f32),
            dma((2, 2)),
            dma((2, chunks, 2, 2)),
            dma((2, chunks, 2, 2)),
            dma((2,)),
            dma((2,)),
            dma((2,)),
            dma((2,)),
            dma((levels, n_tm)),
            dma((levels, n_tm)),
        ],
        compiler_params=pltpu.CompilerParams(
            collective_id=0, has_side_effects=True, vmem_limit_bytes=40 * 1024 * 1024
        ),
        cost_estimate=pl.CostEstimate(flops=10**9, bytes_accessed=4 * 10**6, transcendentals=0),
    )(
        velocity_u.reshape(snaps, cells, width),
        velocity_v.reshape(snaps, cells, width),
        land_sea, bottom_level, spacing_x, spacing_y,
        jnp.asarray(own), jnp.asarray(halo),
    )
    return conversion.reshape(velocity_u.shape), mean_map


def solution(mesh):
    in_specs = (
        P("tm", None, None, "tile"),
        P("tm", None, None, "tile"),
        P(None, "tile"),
        P(None, "tile"),
        P(None, "tile"),
        P(None, "tile"),
    )
    out_specs = (P("tm", None, None, "tile"), P(None, None, "tile"))
    return jax.shard_map(shards, mesh=mesh, in_specs=in_specs, out_specs=out_specs, check_vma=False)
```

time: 267 us -> 71.4 us (0.27); the launches traced: 262 us -> 70.9 us
  local copies, waits for them, and re-layouts: 90.4 us -> 8.65 us
  waiting for transfers between devices: 74.3 us -> 0 us
  Pallas kernels: 0 us -> 61.6 us
  other arithmetic: 29.2 us -> 0 us
  matrix products: 24.2 us -> 0 us
  blocking collectives: 22.3 us -> 0 us
  starting transfers between devices: 15.7 us -> 0 us
  loops' own time: 5.18 us -> 0 us
    all_to_all x2 -> x0, waiting for transfers between devices: 74.3 us -> none  [the longest x1 37.7 us: shards(): lax.all_to_all(series_mean, 'tm', split_axis=0, concat_axis=2, tiled=True)]
    pallas_call x0 -> x1, Pallas kernels: none -> 61.6 us  [shards(): pl.pallas_call(functools.partial(kernel, n_tm, n_tile, levels), out_shape...]
    unnamed x19 -> x18, local copies, waits for them, and re-layouts: 37 us -> 8.65 us
    dot_general x16 -> x0, matrix products: 24.2 us -> none  [the longest x8 16.8 us: one_block(): jnp.dot(matrix, window, precision=lax.Precision.HIGHEST, preferred_elemen...]
    psum x1 -> x0, blocking collectives: 22.3 us -> none  [shards(): summed = lax.psum(jnp.sum(conversion, axis=0), 'tm')]
    another operation x4 -> x0, local copies, waits for them, and re-layouts: 17.7 us -> none  [the longest x3 12.1 us: shards(): stacked = jnp.stack([velocity_u, velocity_v], axis=1)]
    all_to_all x5 -> x0, local copies, waits for them, and re-layouts: 12.8 us -> none  [the longest x3 9.91 us: shards(): lax.all_to_all(flat_cells, 'tm', split_axis=2, concat_axis=0, tiled=True)]
    all_to_all x1 -> x0, other arithmetic: 11.2 us -> none  [shards(): lax.all_to_all(flat_cells, 'tm', split_axis=2, concat_axis=0, tiled=True)]
  transfers between devices with their start and end apart: 4 -> 0, of which waited for: 2 -> 0; matrix products, arithmetic and copies ran while one was open for 3% -> 0% of each run, Pallas kernels for 0% -> 0%
where the time goes in v1:
time: 71.4 us; the launch traced here: 70.9 us
  Pallas kernels  61.6 us (86%)
  local copies, waits for them, and re-layouts  8.65 us (12%)
    pallas_call x1, Pallas kernels, shards(): pl.pallas_call(functools.partial(kernel, n_tm, n_tile, levels), out_shape...  61.6 us
    unnamed x18, local copies, waits for them, and re-layouts  8.65 us

profile of v1, /device:TPU:0, one launch (start us, length us, event | category | flops | bytes accessed | tf_op | source)
XLA Modules:
  0.0 70.9 jit_solution(6760379654830684077)
XLA Ops:
  0.6 0.0 copy-start
  0.6 1.4 %copy-done = f32[48,2,16,256]{3,2,1,0:T(8,128)S(1)} copy-done((f32[48,2,16,256]{3,2,1,0:T(8,128)S(1)}, f32[48,2,16,256]{3,2,1,0:T(8,128)}, u32[]{:S(2)}) %copy-start) | copy-done | bytes 1572888
  2.0 0.0 copy-start.1
  2.0 1.4 %copy-done.1 = f32[48,2,16,256]{3,2,1,0:T(8,128)S(1)} copy-done((f32[48,2,16,256]{3,2,1,0:T(8,128)S(1)}, f32[48,2,16,256]{3,2,1,0:T(8,128)}, u32[]{:S(2)}) %copy-start.1) | copy-done | bytes 1572888
  3.4 0.0 copy-start.2
  3.5 0.7 %copy-done.2 = s32[16,256]{1,0:T(8,128)S(1)} copy-done((s32[16,256]{1,0:T(8,128)S(1)}, s32[16,256]{1,0:T(8,128)}, u32[]{:S(2)}) %copy-start.2) | copy-done | bytes 16408
  4.2 0.0 copy-start.3
  4.2 0.7 %copy-done.3 = s32[16,256]{1,0:T(8,128)S(1)} copy-done((s32[16,256]{1,0:T(8,128)S(1)}, s32[16,256]{1,0:T(8,128)}, u32[]{:S(2)}) %copy-start.3) | copy-done | bytes 16408
  4.9 0.0 copy-start.4
  4.9 0.7 %copy-done.4 = f32[16,256]{1,0:T(8,128)S(1)} copy-done((f32[16,256]{1,0:T(8,128)S(1)}, f32[16,256]{1,0:T(8,128)}, u32[]{:S(2)}) %copy-start.4) | copy-done | bytes 16408
  5.6 0.0 copy-start.5
  5.6 0.7 %copy-done.5 = f32[16,256]{1,0:T(8,128)S(1)} copy-done((f32[16,256]{1,0:T(8,128)S(1)}, f32[16,256]{1,0:T(8,128)}, u32[]{:S(2)}) %copy-start.5) | copy-done | bytes 16408
  6.3 0.0 copy-start.6
  6.3 0.7 %copy-done.6 = f32[48,48]{1,0:T(8,128)S(1)} copy-done((f32[48,48]{1,0:T(8,128)S(1)}, f32[48,48]{1,0:T(8,128)}, u32[]{:S(2)}) %copy-start.6) | copy-done | bytes 9240
  7.1 0.0 copy-start.7
  7.1 0.7 %copy-done.7 = f32[48,48]{1,0:T(8,128)S(1)} copy-done((f32[48,48]{1,0:T(8,128)S(1)}, f32[48,48]{1,0:T(8,128)}, u32[]{:S(2)}) %copy-start.7) | copy-done | bytes 9240
  7.8 61.6 %shard_map.95 = (bf16[48,32,256]{2,1,0:T(8,128)(2,1)S(1)}, f32[2,16,256]{2,1,0:T(8,128)S(1)}) custom-call(f32[48,32,256]{2,1,0:T(8,128)S(1)} %bitcast.4, f32[48,32,256]{2,1,0:T(8,128)S(1)} %bitcast.5, s32[16,256]{1,0:T(8,128)S(1)} %copy-done.2, s32[16,256]{1,0:T(8,128)S(1)} %copy-done.3, f32[16,256]{1,0:T(8,128)S(1)} %copy-done.4, f32[16,256]{1,0:T(8,128)S(1)} %copy-done.5, ...), custom_call_target="tpu_custom_call" | custom-call | flops 1000000000 | bytes 4000000 | tf_op jit(solution)/shard_map/pallas_call | solution.py:335
  69.4 0.9 %copy.12 = bf16[48,2,16,256]{3,2,1,0:T(8,128)(2,1)} copy(bf16[48,2,16,256]{3,2,1,0:T(8,128)(2,1)S(1)} %bitcast.3) | data formatting | bytes 1572864
  70.3 0.6 copy.13
Async XLA Ops:
  0.6 1.4 %copy-start = (f32[48,2,16,256]{3,2,1,0:T(8,128)S(1)}, f32[48,2,16,256]{3,2,1,0:T(8,128)}, u32[]{:S(2)}) copy-start(f32[48,2,16,256]{3,2,1,0:T(8,128)} %param.8) | copy-start | bytes 4718596
  2.0 1.4 %copy-start.1 = (f32[48,2,16,256]{3,2,1,0:T(8,128)S(1)}, f32[48,2,16,256]{3,2,1,0:T(8,128)}, u32[]{:S(2)}) copy-start(f32[48,2,16,256]{3,2,1,0:T(8,128)} %param.9) | copy-start | bytes 4718596
  3.4 0.7 %copy-start.2 = (s32[16,256]{1,0:T(8,128)S(1)}, s32[16,256]{1,0:T(8,128)}, u32[]{:S(2)}) copy-start(s32[16,256]{1,0:T(8,128)} %land_ref.1) | copy-start | bytes 49156
  4.2 0.7 %copy-start.3 = (s32[16,256]{1,0:T(8,128)S(1)}, s32[16,256]{1,0:T(8,128)}, u32[]{:S(2)}) copy-start(s32[16,256]{1,0:T(8,128)} %bottom_ref.1) | copy-start | bytes 49156
  4.9 0.7 %copy-start.4 = (f32[16,256]{1,0:T(8,128)S(1)}, f32[16,256]{1,0:T(8,128)}, u32[]{:S(2)}) copy-start(f32[16,256]{1,0:T(8,128)} %sx_ref.1) | copy-start | bytes 49156
  5.6 0.7 %copy-start.5 = (f32[16,256]{1,0:T(8,128)S(1)}, f32[16,256]{1,0:T(8,128)}, u32[]{:S(2)}) copy-start(f32[16,256]{1,0:T(8,128)} %sy_ref.1) | copy-start | bytes 49156
  6.3 0.7 %copy-start.6 = (f32[48,48]{1,0:T(8,128)S(1)}, f32[48,48]{1,0:T(8,128)}, u32[]{:S(2)}) copy-start(f32[48,48]{1,0:T(8,128)} %constant.5.clone.halo_w_ref) | copy-start | bytes 27652
  7.1 0.7 %copy-start.7 = (f32[48,48]{1,0:T(8,128)S(1)}, f32[48,48]{1,0:T(8,128)}, u32[]{:S(2)}) copy-start(f32[48,48]{1,0:T(8,128)} %constant.4.clone.own_ref) | copy-start | bytes 27652

commit v2 on v1

--- a/solution.py
+++ b/solution.py
@@ -12,6 +12,8 @@
 CUTOFF = 1.0 / 40.0
 LANES = 128
 CHUNK = 8
+DEPTH = 2
+UNROLL = 4
 MESH = pl.DeviceIdType.MESH
 
 
@@ -30,8 +32,9 @@
 
 def kernel(
     n_tm, n_tile, levels,
-    u_ref, v_ref, land_ref, bottom_ref, sx_ref, sy_ref, own_ref, halo_w_ref,
+    u_ref, v_ref, land_in, bottom_in, sx_in, sy_in, own_in, halo_in,
     conv_ref, mean_ref,
+    land_ref, bottom_ref, sx_ref, sy_ref, own_ref, halo_w_ref, small_sem,
     x, halo, mm, cf, wet, cx, cy, sums, part, edge, edge_halo, edge_mean, edge_in,
     x_sem, bulk_send, bulk_recv, edge_send, edge_recv, em_send, em_recv, part_send, part_recv,
 ):
@@ -59,6 +62,12 @@
             fields[f].at[:, :, pl.ds(h * LANES, LANES)], x.at[f, h], x_sem.at[f, h]
         )
 
+    small = (
+        (land_in, land_ref), (bottom_in, bottom_ref), (sx_in, sx_ref),
+        (sy_in, sy_ref), (own_in, own_ref), (halo_in, halo_w_ref),
+    )
+    for i, (src, dst) in enumerate(small):
+        pltpu.make_async_copy(src, dst, small_sem.at[i]).start()
     for f in range(2):
         for h in range(2):
             local(f, h).start()
@@ -115,7 +124,7 @@
     z_sends = (z < n_tile - 1, z > 0)
     z_receives = (z > 0, z < n_tile - 1)
 
-    for c in range(chunks):
+    def start_chunk(c):
         for side in range(2):
 
             @pl.when(sends[side])
@@ -124,6 +133,18 @@
                     for h in range(2):
                         bulk(side, c, f, h).start()
 
+    def finish_chunk(c):
+        for side in range(2):
+
+            @pl.when(sends[side])
+            def _():
+                for f in range(2):
+                    for h in range(2):
+                        bulk(side, c, f, h).wait_send()
+
+    for c in range(DEPTH):
+        start_chunk(c)
+
     for side in range(2):
 
         @pl.when(jnp.logical_not(receives[side]))
@@ -134,6 +155,9 @@
         @pl.when(jnp.logical_not(z_receives[side]))
         def _():
             edge_in[side] = jnp.zeros(edge_in.shape[1:], jnp.float32)
+
+    for i, (src, dst) in enumerate(small):
+        pltpu.make_async_copy(src, dst, small_sem.at[i]).wait()
 
     for l in range(levels):
         is_wet = (land_ref[...] == 1) & (l < bottom_ref[...])
@@ -189,7 +213,7 @@
             mm[f, l, j + 1] = dot(own_w, block)
         return carry
 
-    lax.fori_loop(0, cells, own_part, 0)
+    lax.fori_loop(0, cells, own_part, 0, unroll=UNROLL)
 
     for side in range(2):
 
@@ -260,6 +284,9 @@
 
     per_level = rows // CHUNK
     for c in range(chunks):
+        finish_chunk(c)
+        if c + DEPTH < chunks:
+            start_chunk(c + DEPTH)
         for side in range(2):
 
             @pl.when(receives[side])
@@ -268,7 +295,7 @@
                     for h in range(2):
                         bulk(side, c, f, h).wait_recv()
 
-        lax.fori_loop(c * CHUNK, (c + 1) * CHUNK, halo_part, 0)
+        lax.fori_loop(c * CHUNK, (c + 1) * CHUNK, halo_part, 0, unroll=UNROLL)
         if c == 0:
             for side in range(2):
 
@@ -307,10 +334,6 @@
         @pl.when(sends[side])
         def _():
             edge_copy(side).wait_send()
-            for c in range(chunks):
-                for f in range(2):
-                    for h in range(2):
-                        bulk(side, c, f, h).wait_send()
 
         @pl.when(z_sends[side])
         def _():
@@ -329,7 +352,7 @@
     own, halo = band_parts(snaps)
     chunks = cells // CHUNK
     vmem = pl.BlockSpec(memory_space=pltpu.VMEM)
-    anywhere = pl.BlockSpec(memory_space=pl.ANY)
+    hbm = pl.BlockSpec(memory_space=pltpu.HBM)
     f32 = jnp.float32
     dma = pltpu.SemaphoreType.DMA
     conversion, mean_map = pl.pallas_call(
@@ -338,9 +361,16 @@
             jax.ShapeDtypeStruct((snaps, cells, width), jnp.bfloat16),
             jax.ShapeDtypeStruct((levels, rows, width), f32),
         ),
-        in_specs=[anywhere] * 2 + [vmem] * 6,
+        in_specs=[hbm] * 8,
         out_specs=(vmem, vmem),
         scratch_shapes=[
+            pltpu.VMEM((rows, width), jnp.int32),
+            pltpu.VMEM((rows, width), jnp.int32),
+            pltpu.VMEM((rows, width), f32),
+            pltpu.VMEM((rows, width), f32),
+            pltpu.VMEM(own.shape, f32),
+            pltpu.VMEM(halo.shape, f32),
+            dma((6,)),
             pltpu.VMEM((2, 2, snaps, cells, LANES), f32),
             pltpu.VMEM((2, 2, 2, HALF, cells, LANES), f32),
             pltpu.VMEM((2, levels, rows + 2, snaps, width), f32),

time: 71.4 us -> 57.5 us (0.81)
  Pallas kernels: 61.6 us -> 47.7 us
    pallas_call x1, Pallas kernels: 61.6 us -> 47.7 us  [shards(): pl.pallas_call(functools.partial(kernel, n_tm, n_tile, levels), out_shape...]
where the time goes in v2:
time: 57.5 us; the launch traced here: 57 us
  Pallas kernels  47.7 us (83%)
  local copies, waits for them, and re-layouts  8.65 us (15%)
  between operations  0.66 us (1%)
    pallas_call x1, Pallas kernels, shards(): pl.pallas_call(functools.partial(kernel, n_tm, n_tile, levels), out_shape...  47.7 us
    unnamed x18, local copies, waits for them, and re-layouts  8.65 us

profile of v2, /device:TPU:0, one launch (start us, length us, event | category | flops | bytes accessed | tf_op | source)
XLA Modules:
  0.0 57.0 jit_solution(8559078015290551327)
XLA Ops:
  0.6 0.0 copy-start
  0.6 1.4 %copy-done = f32[48,2,16,256]{3,2,1,0:T(8,128)S(1)} copy-done((f32[48,2,16,256]{3,2,1,0:T(8,128)S(1)}, f32[48,2,16,256]{3,2,1,0:T(8,128)}, u32[]{:S(2)}) %copy-start) | copy-done | bytes 1572888
  2.0 0.0 copy-start.1
  2.0 1.4 %copy-done.1 = f32[48,2,16,256]{3,2,1,0:T(8,128)S(1)} copy-done((f32[48,2,16,256]{3,2,1,0:T(8,128)S(1)}, f32[48,2,16,256]{3,2,1,0:T(8,128)}, u32[]{:S(2)}) %copy-start.1) | copy-done | bytes 1572888
  3.4 0.0 copy-start.2
  3.5 0.7 %copy-done.2 = s32[16,256]{1,0:T(8,128)S(1)} copy-done((s32[16,256]{1,0:T(8,128)S(1)}, s32[16,256]{1,0:T(8,128)}, u32[]{:S(2)}) %copy-start.2) | copy-done | bytes 16408
  4.2 0.0 copy-start.3
  4.2 0.7 %copy-done.3 = s32[16,256]{1,0:T(8,128)S(1)} copy-done((s32[16,256]{1,0:T(8,128)S(1)}, s32[16,256]{1,0:T(8,128)}, u32[]{:S(2)}) %copy-start.3) | copy-done | bytes 16408
  4.9 0.0 copy-start.4
  4.9 0.7 %copy-done.4 = f32[16,256]{1,0:T(8,128)S(1)} copy-done((f32[16,256]{1,0:T(8,128)S(1)}, f32[16,256]{1,0:T(8,128)}, u32[]{:S(2)}) %copy-start.4) | copy-done | bytes 16408
  5.6 0.0 copy-start.5
  5.6 0.7 %copy-done.5 = f32[16,256]{1,0:T(8,128)S(1)} copy-done((f32[16,256]{1,0:T(8,128)S(1)}, f32[16,256]{1,0:T(8,128)}, u32[]{:S(2)}) %copy-start.5) | copy-done | bytes 16408
  6.3 0.0 copy-start.6
  6.3 0.7 %copy-done.6 = f32[48,48]{1,0:T(8,128)S(1)} copy-done((f32[48,48]{1,0:T(8,128)S(1)}, f32[48,48]{1,0:T(8,128)}, u32[]{:S(2)}) %copy-start.6) | copy-done | bytes 9240
  7.1 0.0 copy-start.7
  7.1 0.7 %copy-done.7 = f32[48,48]{1,0:T(8,128)S(1)} copy-done((f32[48,48]{1,0:T(8,128)S(1)}, f32[48,48]{1,0:T(8,128)}, u32[]{:S(2)}) %copy-start.7) | copy-done | bytes 9240
  7.8 47.7 %shard_map.95 = (bf16[48,32,256]{2,1,0:T(8,128)(2,1)S(1)}, f32[2,16,256]{2,1,0:T(8,128)S(1)}) custom-call(f32[48,32,256]{2,1,0:T(8,128)S(1)} %bitcast.4, f32[48,32,256]{2,1,0:T(8,128)S(1)} %bitcast.5, s32[16,256]{1,0:T(8,128)S(1)} %copy-done.2, s32[16,256]{1,0:T(8,128)S(1)} %copy-done.3, f32[16,256]{1,0:T(8,128)S(1)} %copy-done.4, f32[16,256]{1,0:T(8,128)S(1)} %copy-done.5, ...), custom_call_target="tpu_custom_call" | custom-call | flops 1000000000 | bytes 4000000 | tf_op jit(solution)/shard_map/pallas_call | solution.py:358
  55.5 0.9 %copy.12 = bf16[48,2,16,256]{3,2,1,0:T(8,128)(2,1)} copy(bf16[48,2,16,256]{3,2,1,0:T(8,128)(2,1)S(1)} %bitcast.3) | data formatting | bytes 1572864
  56.4 0.6 %copy.13 = f32[2,16,256]{2,1,0:T(8,128)} copy(f32[2,16,256]{2,1,0:T(8,128)S(1)} %get-tuple-element.9) | data formatting | bytes 65536
Async XLA Ops:
  0.6 1.4 %copy-start = (f32[48,2,16,256]{3,2,1,0:T(8,128)S(1)}, f32[48,2,16,256]{3,2,1,0:T(8,128)}, u32[]{:S(2)}) copy-start(f32[48,2,16,256]{3,2,1,0:T(8,128)} %param.8) | copy-start | bytes 4718596
  2.0 1.4 %copy-start.1 = (f32[48,2,16,256]{3,2,1,0:T(8,128)S(1)}, f32[48,2,16,256]{3,2,1,0:T(8,128)}, u32[]{:S(2)}) copy-start(f32[48,2,16,256]{3,2,1,0:T(8,128)} %param.9) | copy-start | bytes 4718596
  3.4 0.7 %copy-start.2 = (s32[16,256]{1,0:T(8,128)S(1)}, s32[16,256]{1,0:T(8,128)}, u32[]{:S(2)}) copy-start(s32[16,256]{1,0:T(8,128)} %land_in.1) | copy-start | bytes 49156
  4.2 0.7 %copy-start.3 = (s32[16,256]{1,0:T(8,128)S(1)}, s32[16,256]{1,0:T(8,128)}, u32[]{:S(2)}) copy-start(s32[16,256]{1,0:T(8,128)} %bottom_in.1) | copy-start | bytes 49156
  4.9 0.7 %copy-start.4 = (f32[16,256]{1,0:T(8,128)S(1)}, f32[16,256]{1,0:T(8,128)}, u32[]{:S(2)}) copy-start(f32[16,256]{1,0:T(8,128)} %sx_in.1) | copy-start | bytes 49156
  5.6 0.7 %copy-start.5 = (f32[16,256]{1,0:T(8,128)S(1)}, f32[16,256]{1,0:T(8,128)}, u32[]{:S(2)}) copy-start(f32[16,256]{1,0:T(8,128)} %sy_in.1) | copy-start | bytes 49156
  6.3 0.7 %copy-start.6 = (f32[48,48]{1,0:T(8,128)S(1)}, f32[48,48]{1,0:T(8,128)}, u32[]{:S(2)}) copy-start(f32[48,48]{1,0:T(8,128)} %constant.5.clone.halo_in) | copy-start | bytes 27652
  7.1 0.7 %copy-start.7 = (f32[48,48]{1,0:T(8,128)S(1)}, f32[48,48]{1,0:T(8,128)}, u32[]{:S(2)}) copy-start(f32[48,48]{1,0:T(8,128)} %constant.4.clone.own_in) | copy-start | bytes 27652

commit v3 on v2

--- a/solution.py
+++ b/solution.py
@@ -36,6 +36,7 @@
     conv_ref, mean_ref,
     land_ref, bottom_ref, sx_ref, sy_ref, own_ref, halo_w_ref, small_sem,
     x, halo, mm, cf, wet, cx, cy, sums, part, edge, edge_halo, edge_mean, edge_in,
+    relayed, relay_send, relay_recv,
     x_sem, bulk_send, bulk_recv, edge_send, edge_recv, em_send, em_recv, part_send, part_recv,
 ):
     snaps, cells, width = u_ref.shape
@@ -86,6 +87,41 @@
             device_id_type=MESH,
         )
 
+    middle = (n_tm // 2 - 1, n_tm // 2)
+    via = (n_tm - 1, 0)
+
+    def to_relay(side, c, h):
+        first = snaps - HALF if side == 0 else 0
+        return pltpu.make_async_remote_copy(
+            src_ref=fields[1].at[pl.ds(first, HALF), pl.ds(c * CHUNK, CHUNK), pl.ds(h * LANES, LANES)],
+            dst_ref=relayed.at[c, h],
+            send_sem=bulk_send.at[side, c, 1, h],
+            recv_sem=relay_recv.at[c, h],
+            device_id={"tm": via[side]},
+            device_id_type=MESH,
+        )
+
+    def from_relay(side, c, h):
+        return pltpu.make_async_remote_copy(
+            src_ref=relayed.at[c, h],
+            dst_ref=halo.at[side, 1, h, :, pl.ds(c * CHUNK, CHUNK), :],
+            send_sem=relay_send.at[c, h],
+            recv_sem=bulk_recv.at[side, c, 1, h],
+            device_id={"tm": middle[1 - side]},
+            device_id_type=MESH,
+        )
+
+    def pass_on(c):
+        if n_tm < 4:
+            return
+        for side in range(2):
+
+            @pl.when(t == via[side])
+            def _():
+                for h in range(2):
+                    to_relay(side, c, h).wait_recv()
+                    from_relay(side, c, h).start()
+
     def edge_copy(side):
         first = snaps - HALF if side == 0 else 0
         to = t + 1 if side == 0 else t - 1
@@ -127,7 +163,19 @@
     def start_chunk(c):
         for side in range(2):
 
-            @pl.when(sends[side])
+            if n_tm >= 4:
+
+                @pl.when(t == middle[side])
+                def _():
+                    for h in range(2):
+                        to_relay(side, c, h).start()
+                        bulk(side, c, 0, h).start()
+
+                whole = sends[side] & (t != middle[side])
+            else:
+                whole = sends[side]
+
+            @pl.when(whole)
             def _():
                 for f in range(2):
                     for h in range(2):
@@ -199,12 +247,14 @@
             acc = jnp.where(lane == q, pltpu.roll(last, lax.rem(q + 1, LANES), 1), acc)
         return acc
 
-    edge[...] = lax.fori_loop(0, cells, pack, jnp.zeros((snaps, LANES), jnp.float32))
+    edge[...] = lax.fori_loop(0, cells, pack, jnp.zeros((snaps, LANES), jnp.float32), unroll=UNROLL)
     for side in range(2):
 
         @pl.when(sends[side])
         def _():
             edge_copy(side).start()
+
+    pass_on(0)
 
     def own_part(r, carry):
         l, j = r // rows, lax.rem(r, rows)
@@ -214,6 +264,8 @@
         return carry
 
     lax.fori_loop(0, cells, own_part, 0, unroll=UNROLL)
+    for c in range(1, DEPTH):
+        pass_on(c)
 
     for side in range(2):
 
@@ -306,7 +358,9 @@
         l, piece = c // per_level, c % per_level
         low = piece * CHUNK - (1 if piece else 0)
         high = rows if piece == per_level - 1 else (piece + 1) * CHUNK - 1
-        lax.fori_loop(low, high, convert(l), 0)
+        lax.fori_loop(low, high, convert(l), 0, unroll=2)
+        if c + DEPTH < chunks:
+            pass_on(c + DEPTH)
         if piece == per_level - 1:
             part[t, l] = jnp.concatenate([sums[l * rows + j] for j in range(rows)], axis=0)
             for k in range(1, n_tm):
@@ -338,6 +392,14 @@
         @pl.when(z_sends[side])
         def _():
             mean_copy(side).wait_send()
+
+        if n_tm >= 4:
+
+            @pl.when(t == via[side])
+            def _():
+                for c in range(chunks):
+                    for h in range(2):
+                        from_relay(side, c, h).wait_send()
 
     for l in range(levels):
         for k in range(1, n_tm):
@@ -384,6 +446,9 @@
             pltpu.VMEM((2, HALF, LANES), f32),
             pltpu.VMEM((snaps, LANES), f32),
             pltpu.VMEM((2, snaps, LANES), f32),
+            pltpu.VMEM((chunks, 2, HALF, CHUNK, LANES), f32),
+            dma((chunks, 2)),
+            dma((chunks, 2)),
             dma((2, 2)),
             dma((2, chunks, 2, 2)),
             dma((2, chunks, 2, 2)),

time: 57.5 us -> 52.7 us (0.917)
  Pallas kernels: 47.7 us -> 42.9 us
    pallas_call x1, Pallas kernels: 47.7 us -> 42.9 us  [shards(): pl.pallas_call(functools.partial(kernel, n_tm, n_tile, levels), out_shape...]
where the time goes in v3:
time: 52.7 us; the launch traced here: 52.2 us
  Pallas kernels  42.9 us (81%)
  local copies, waits for them, and re-layouts  8.65 us (16%)
  between operations  0.66 us (1%)
    pallas_call x1, Pallas kernels, shards(): pl.pallas_call(functools.partial(kernel, n_tm, n_tile, levels), out_shape...  42.9 us
    unnamed x18, local copies, waits for them, and re-layouts  8.65 us

profile of v3, /device:TPU:0, one launch (start us, length us, event | category | flops | bytes accessed | tf_op | source)
XLA Modules:
  0.0 52.2 jit_solution(3095944840280976032)
XLA Ops:
  0.6 0.0 copy-start
  0.6 1.4 %copy-done = f32[48,2,16,256]{3,2,1,0:T(8,128)S(1)} copy-done((f32[48,2,16,256]{3,2,1,0:T(8,128)S(1)}, f32[48,2,16,256]{3,2,1,0:T(8,128)}, u32[]{:S(2)}) %copy-start) | copy-done | bytes 1572888
  2.0 0.0 copy-start.1
  2.0 1.4 %copy-done.1 = f32[48,2,16,256]{3,2,1,0:T(8,128)S(1)} copy-done((f32[48,2,16,256]{3,2,1,0:T(8,128)S(1)}, f32[48,2,16,256]{3,2,1,0:T(8,128)}, u32[]{:S(2)}) %copy-start.1) | copy-done | bytes 1572888
  3.4 0.0 copy-start.2
  3.5 0.7 %copy-done.2 = s32[16,256]{1,0:T(8,128)S(1)} copy-done((s32[16,256]{1,0:T(8,128)S(1)}, s32[16,256]{1,0:T(8,128)}, u32[]{:S(2)}) %copy-start.2) | copy-done | bytes 16408
  4.2 0.0 copy-start.3
  4.2 0.7 %copy-done.3 = s32[16,256]{1,0:T(8,128)S(1)} copy-done((s32[16,256]{1,0:T(8,128)S(1)}, s32[16,256]{1,0:T(8,128)}, u32[]{:S(2)}) %copy-start.3) | copy-done | bytes 16408
  4.9 0.0 copy-start.4
  4.9 0.7 %copy-done.4 = f32[16,256]{1,0:T(8,128)S(1)} copy-done((f32[16,256]{1,0:T(8,128)S(1)}, f32[16,256]{1,0:T(8,128)}, u32[]{:S(2)}) %copy-start.4) | copy-done | bytes 16408
  5.6 0.0 copy-start.5
  5.6 0.7 %copy-done.5 = f32[16,256]{1,0:T(8,128)S(1)} copy-done((f32[16,256]{1,0:T(8,128)S(1)}, f32[16,256]{1,0:T(8,128)}, u32[]{:S(2)}) %copy-start.5) | copy-done | bytes 16408
  6.3 0.0 copy-start.6
  6.3 0.7 %copy-done.6 = f32[48,48]{1,0:T(8,128)S(1)} copy-done((f32[48,48]{1,0:T(8,128)S(1)}, f32[48,48]{1,0:T(8,128)}, u32[]{:S(2)}) %copy-start.6) | copy-done | bytes 9240
  7.1 0.0 copy-start.7
  7.1 0.7 %copy-done.7 = f32[48,48]{1,0:T(8,128)S(1)} copy-done((f32[48,48]{1,0:T(8,128)S(1)}, f32[48,48]{1,0:T(8,128)}, u32[]{:S(2)}) %copy-start.7) | copy-done | bytes 9240
  7.8 42.9 %shard_map.95 = (bf16[48,32,256]{2,1,0:T(8,128)(2,1)S(1)}, f32[2,16,256]{2,1,0:T(8,128)S(1)}) custom-call(f32[48,32,256]{2,1,0:T(8,128)S(1)} %bitcast.4, f32[48,32,256]{2,1,0:T(8,128)S(1)} %bitcast.5, s32[16,256]{1,0:T(8,128)S(1)} %copy-done.2, s32[16,256]{1,0:T(8,128)S(1)} %copy-done.3, f32[16,256]{1,0:T(8,128)S(1)} %copy-done.4, f32[16,256]{1,0:T(8,128)S(1)} %copy-done.5, ...), custom_call_target="tpu_custom_call" | custom-call | flops 1000000000 | bytes 4000000 | tf_op jit(solution)/shard_map/pallas_call | solution.py:420
  50.7 0.9 %copy.12 = bf16[48,2,16,256]{3,2,1,0:T(8,128)(2,1)} copy(bf16[48,2,16,256]{3,2,1,0:T(8,128)(2,1)S(1)} %bitcast.3) | data formatting | bytes 1572864
  51.6 0.6 %copy.13 = f32[2,16,256]{2,1,0:T(8,128)} copy(f32[2,16,256]{2,1,0:T(8,128)S(1)} %get-tuple-element.9) | data formatting | bytes 65536
Async XLA Ops:
  0.6 1.4 %copy-start = (f32[48,2,16,256]{3,2,1,0:T(8,128)S(1)}, f32[48,2,16,256]{3,2,1,0:T(8,128)}, u32[]{:S(2)}) copy-start(f32[48,2,16,256]{3,2,1,0:T(8,128)} %param.8) | copy-start | bytes 4718596
  2.0 1.4 %copy-start.1 = (f32[48,2,16,256]{3,2,1,0:T(8,128)S(1)}, f32[48,2,16,256]{3,2,1,0:T(8,128)}, u32[]{:S(2)}) copy-start(f32[48,2,16,256]{3,2,1,0:T(8,128)} %param.9) | copy-start | bytes 4718596
  3.4 0.7 %copy-start.2 = (s32[16,256]{1,0:T(8,128)S(1)}, s32[16,256]{1,0:T(8,128)}, u32[]{:S(2)}) copy-start(s32[16,256]{1,0:T(8,128)} %land_in.1) | copy-start | bytes 49156
  4.2 0.7 %copy-start.3 = (s32[16,256]{1,0:T(8,128)S(1)}, s32[16,256]{1,0:T(8,128)}, u32[]{:S(2)}) copy-start(s32[16,256]{1,0:T(8,128)} %bottom_in.1) | copy-start | bytes 49156
  4.9 0.7 %copy-start.4 = (f32[16,256]{1,0:T(8,128)S(1)}, f32[16,256]{1,0:T(8,128)}, u32[]{:S(2)}) copy-start(f32[16,256]{1,0:T(8,128)} %sx_in.1) | copy-start | bytes 49156
  5.6 0.7 %copy-start.5 = (f32[16,256]{1,0:T(8,128)S(1)}, f32[16,256]{1,0:T(8,128)}, u32[]{:S(2)}) copy-start(f32[16,256]{1,0:T(8,128)} %sy_in.1) | copy-start | bytes 49156
  6.3 0.7 %copy-start.6 = (f32[48,48]{1,0:T(8,128)S(1)}, f32[48,48]{1,0:T(8,128)}, u32[]{:S(2)}) copy-start(f32[48,48]{1,0:T(8,128)} %constant.5.clone.halo_in) | copy-start | bytes 27652
  7.1 0.7 %copy-start.7 = (f32[48,48]{1,0:T(8,128)S(1)}, f32[48,48]{1,0:T(8,128)}, u32[]{:S(2)}) copy-start(f32[48,48]{1,0:T(8,128)} %constant.4.clone.own_in) | copy-start | bytes 27652

commit v4 on v3

--- a/solution.py
+++ b/solution.py
@@ -348,6 +348,8 @@
                         bulk(side, c, f, h).wait_recv()
 
         lax.fori_loop(c * CHUNK, (c + 1) * CHUNK, halo_part, 0, unroll=UNROLL)
+        if c + DEPTH < chunks:
+            pass_on(c + DEPTH)
         if c == 0:
             for side in range(2):
 
@@ -359,8 +361,6 @@
         low = piece * CHUNK - (1 if piece else 0)
         high = rows if piece == per_level - 1 else (piece + 1) * CHUNK - 1
         lax.fori_loop(low, high, convert(l), 0, unroll=2)
-        if c + DEPTH < chunks:
-            pass_on(c + DEPTH)
         if piece == per_level - 1:
             part[t, l] = jnp.concatenate([sums[l * rows + j] for j in range(rows)], axis=0)
             for k in range(1, n_tm):

time: 52.7 us -> 51.1 us (0.970)
  Pallas kernels: 42.9 us -> 41.3 us
    pallas_call x1, Pallas kernels: 42.9 us -> 41.3 us  [shards(): pl.pallas_call(functools.partial(kernel, n_tm, n_tile, levels), out_shape...]
where the time goes in v4:
time: 51.1 us; the launch traced here: 50.6 us
  Pallas kernels  41.3 us (81%)
  local copies, waits for them, and re-layouts  8.65 us (17%)
  between operations  0.66 us (1%)
    pallas_call x1, Pallas kernels, shards(): pl.pallas_call(functools.partial(kernel, n_tm, n_tile, levels), out_shape...  41.3 us
    unnamed x18, local copies, waits for them, and re-layouts  8.65 us

profile of v4, /device:TPU:0, one launch (start us, length us, event | category | flops | bytes accessed | tf_op | source)
XLA Modules:
  0.0 50.6 jit_solution(15017090910374728919)
XLA Ops:
  0.6 0.0 copy-start
  0.6 1.4 %copy-done = f32[48,2,16,256]{3,2,1,0:T(8,128)S(1)} copy-done((f32[48,2,16,256]{3,2,1,0:T(8,128)S(1)}, f32[48,2,16,256]{3,2,1,0:T(8,128)}, u32[]{:S(2)}) %copy-start) | copy-done | bytes 1572888
  2.0 0.0 copy-start.1
  2.0 1.4 %copy-done.1 = f32[48,2,16,256]{3,2,1,0:T(8,128)S(1)} copy-done((f32[48,2,16,256]{3,2,1,0:T(8,128)S(1)}, f32[48,2,16,256]{3,2,1,0:T(8,128)}, u32[]{:S(2)}) %copy-start.1) | copy-done | bytes 1572888
  3.4 0.0 copy-start.2
  3.5 0.7 %copy-done.2 = s32[16,256]{1,0:T(8,128)S(1)} copy-done((s32[16,256]{1,0:T(8,128)S(1)}, s32[16,256]{1,0:T(8,128)}, u32[]{:S(2)}) %copy-start.2) | copy-done | bytes 16408
  4.2 0.0 copy-start.3
  4.2 0.7 %copy-done.3 = s32[16,256]{1,0:T(8,128)S(1)} copy-done((s32[16,256]{1,0:T(8,128)S(1)}, s32[16,256]{1,0:T(8,128)}, u32[]{:S(2)}) %copy-start.3) | copy-done | bytes 16408
  4.9 0.0 copy-start.4
  4.9 0.7 %copy-done.4 = f32[16,256]{1,0:T(8,128)S(1)} copy-done((f32[16,256]{1,0:T(8,128)S(1)}, f32[16,256]{1,0:T(8,128)}, u32[]{:S(2)}) %copy-start.4) | copy-done | bytes 16408
  5.6 0.0 copy-start.5
  5.6 0.7 %copy-done.5 = f32[16,256]{1,0:T(8,128)S(1)} copy-done((f32[16,256]{1,0:T(8,128)S(1)}, f32[16,256]{1,0:T(8,128)}, u32[]{:S(2)}) %copy-start.5) | copy-done | bytes 16408
  6.3 0.0 copy-start.6
  6.3 0.7 %copy-done.6 = f32[48,48]{1,0:T(8,128)S(1)} copy-done((f32[48,48]{1,0:T(8,128)S(1)}, f32[48,48]{1,0:T(8,128)}, u32[]{:S(2)}) %copy-start.6) | copy-done | bytes 9240
  7.1 0.0 copy-start.7
  7.1 0.7 %copy-done.7 = f32[48,48]{1,0:T(8,128)S(1)} copy-done((f32[48,48]{1,0:T(8,128)S(1)}, f32[48,48]{1,0:T(8,128)}, u32[]{:S(2)}) %copy-start.7) | copy-done | bytes 9240
  7.8 41.3 %shard_map.95 = (bf16[48,32,256]{2,1,0:T(8,128)(2,1)S(1)}, f32[2,16,256]{2,1,0:T(8,128)S(1)}) custom-call(f32[48,32,256]{2,1,0:T(8,128)S(1)} %bitcast.4, f32[48,32,256]{2,1,0:T(8,128)S(1)} %bitcast.5, s32[16,256]{1,0:T(8,128)S(1)} %copy-done.2, s32[16,256]{1,0:T(8,128)S(1)} %copy-done.3, f32[16,256]{1,0:T(8,128)S(1)} %copy-done.4, f32[16,256]{1,0:T(8,128)S(1)} %copy-done.5, ...), custom_call_target="tpu_custom_call" | custom-call | flops 1000000000 | bytes 4000000 | tf_op jit(solution)/shard_map/pallas_call | solution.py:420
  49.1 0.9 %copy.12 = bf16[48,2,16,256]{3,2,1,0:T(8,128)(2,1)} copy(bf16[48,2,16,256]{3,2,1,0:T(8,128)(2,1)S(1)} %bitcast.3) | data formatting | bytes 1572864
  50.0 0.6 %copy.13 = f32[2,16,256]{2,1,0:T(8,128)} copy(f32[2,16,256]{2,1,0:T(8,128)S(1)} %get-tuple-element.9) | data formatting | bytes 65536
Async XLA Ops:
  0.6 1.4 %copy-start = (f32[48,2,16,256]{3,2,1,0:T(8,128)S(1)}, f32[48,2,16,256]{3,2,1,0:T(8,128)}, u32[]{:S(2)}) copy-start(f32[48,2,16,256]{3,2,1,0:T(8,128)} %param.8) | copy-start | bytes 4718596
  2.0 1.4 %copy-start.1 = (f32[48,2,16,256]{3,2,1,0:T(8,128)S(1)}, f32[48,2,16,256]{3,2,1,0:T(8,128)}, u32[]{:S(2)}) copy-start(f32[48,2,16,256]{3,2,1,0:T(8,128)} %param.9) | copy-start | bytes 4718596
  3.4 0.7 %copy-start.2 = (s32[16,256]{1,0:T(8,128)S(1)}, s32[16,256]{1,0:T(8,128)}, u32[]{:S(2)}) copy-start(s32[16,256]{1,0:T(8,128)} %land_in.1) | copy-start | bytes 49156
  4.2 0.7 %copy-start.3 = (s32[16,256]{1,0:T(8,128)S(1)}, s32[16,256]{1,0:T(8,128)}, u32[]{:S(2)}) copy-start(s32[16,256]{1,0:T(8,128)} %bottom_in.1) | copy-start | bytes 49156
  4.9 0.7 %copy-start.4 = (f32[16,256]{1,0:T(8,128)S(1)}, f32[16,256]{1,0:T(8,128)}, u32[]{:S(2)}) copy-start(f32[16,256]{1,0:T(8,128)} %sx_in.1) | copy-start | bytes 49156
  5.6 0.7 %copy-start.5 = (f32[16,256]{1,0:T(8,128)S(1)}, f32[16,256]{1,0:T(8,128)}, u32[]{:S(2)}) copy-start(f32[16,256]{1,0:T(8,128)} %sy_in.1) | copy-start | bytes 49156
  6.3 0.7 %copy-start.6 = (f32[48,48]{1,0:T(8,128)S(1)}, f32[48,48]{1,0:T(8,128)}, u32[]{:S(2)}) copy-start(f32[48,48]{1,0:T(8,128)} %constant.5.clone.halo_in) | copy-start | bytes 27652
  7.1 0.7 %copy-start.7 = (f32[48,48]{1,0:T(8,128)S(1)}, f32[48,48]{1,0:T(8,128)}, u32[]{:S(2)}) copy-start(f32[48,48]{1,0:T(8,128)} %constant.4.clone.own_in) | copy-start | bytes 27652
